TPU v7x, 32 devices: a whole 2x2x4 slice. The times are simulated.
32 devices in a mesh: section: 4 (over z), dp: 2 (over x), fsdp: 4 (over y, core).
Axes of the slice: x: 2, y: 2, z: 4, core: 2. Of those that a mesh axis runs over, the one named last changes fastest.
Arguments:
- x_down: bfloat16 [4, 2, 512, 6144], P('section', 'dp', 'fsdp'), may hold values from -6 to 6
- x_up: bfloat16 [4, 2, 512, 6144], P('section', 'dp', 'fsdp'), may hold values from -6 to 6
- w_tiles: bfloat16 [4, 2, 20, 2, 128, 128], P('section', None, 'fsdp'), as said below
- tile_rows: int32 [4, 2, 20], P('section'), may hold values from 0 to 47, as said below
- tile_cols: int32 [4, 2, 20], P('section'), may hold values from 0 to 191, as said below
- counts: int32 [4, 2, 4], P('section'), may hold values from 2 to 5, as said below
Outputs:
- tile_grads: bfloat16 [4, 20, 2, 128, 128], P('section', 'fsdp')
Inputs may be any that keep to these rules, and one draw needn't show every extreme that they name: w_tiles[l, 1] equals w_tiles[(l + 2) mod 4, 0]. tile_rows[l, 1] equals tile_rows[(l + 2) mod 4, 0]; the 20 row blocks of one layer are distinct. tile_cols[l, 1] equals tile_cols[(l + 2) mod 4, 0]; every column block that a layer uses is used by exactly two of its slots. counts[l, 1] equals counts[(l + 2) mod 4, 0]; the counts of one layer are the numbers 5 - i * 5 // 4 for i < 4 in some order.
All inputs are finite; a program needn't handle non-finite values.
Results may differ from a plain program's by a relative error of at most 0.0065.
Values may be sent and summed in bfloat16 or wider, within the bound.
No kernel may reach another device: no remote copies, remote signals or barrier semaphores. Data moves between devices by JAX's collectives and lax.ppermute only.
A program may use at most 64 MiB of HBM per device.

v0:
```python
import functools
import itertools
import math

import jax
import jax.numpy as jnp
from jax import lax
from jax.experimental import pallas as pl
from jax.experimental.pallas import tpu as pltpu
from jax.sharding import PartitionSpec as P

TILE = 128
PLANE = ("dp", "fsdp")
SOURCES_AT_ONCE = 8
COLUMNS = 192
CORES = 2
COPIES = 4
IN_VMEM = pltpu.CompilerParams(vmem_limit_bytes=16 * 1024 * 1024)

tanh_scale = math.sqrt(2.0 / math.pi)
cubic_coef = 0.044715


def gelu_pair(hidden):
    square = hidden * hidden
    tangent = jnp.tanh(tanh_scale * (hidden + cubic_coef * hidden * square))
    half = 0.5 * (1.0 + tangent)
    value = hidden * half
    slope = half + 0.5 * hidden * (1.0 - tangent * tangent) * tanh_scale * (
        1.0 + 3.0 * cubic_coef * square
    )
    return (value, slope)


def live_total(slots, owners):
    cap = slots // owners
    return sum(cap - i * cap // owners for i in range(owners))


def unit_place(unit, per_half, owners):
    half, at = unit // per_half, unit % per_half
    return at // CORES * owners + half * CORES + at % CORES


def unit_here(per_half, owners):
    owner = lax.axis_index("fsdp")
    at = lax.axis_index("dp") * CORES + owner % CORES
    return owner // CORES * per_half + jnp.minimum(at, per_half - 1)


def order_units(
    cols_ref, counts_ref, which, slots, per_half, order_ref, flags_ref, first_ref, last_ref
):
    per_owner, middle, unused = slots // counts_ref.shape[2], slots // 2, 4 * per_half
    for i in range(order_ref.shape[1]):
        order_ref[which, i] = -1
        flags_ref[which, i] = 0
    cols = []
    for s in range(slots):
        living = counts_ref[0, which, s // per_owner] > s % per_owner
        cols.append(jnp.where(living, cols_ref[0, which, s], COLUMNS))
    yield
    for s in range(slots):
        last_ref[cols[s]] = s
        first_ref[cols[slots - 1 - s]] = slots - 1 - s
    yield
    filled = [jnp.int32(0), jnp.int32(0)]

    def put(unit, slot_a, slot_b, coupled, really):
        at = jnp.where(really, 2 * unit, unused)
        order_ref[which, at] = slot_a
        order_ref[which, at + 1] = slot_b
        flags_ref[which, at] = coupled

    count = lambda condition: jnp.where(condition, 1, 0)
    alone, mixed = [], []
    for s in range(slots):
        living = cols[s] < COLUMNS
        first, last = first_ref[cols[s]], last_ref[cols[s]]
        leads = living & (first == s) & (last > s)
        alone.append(living & (first == last))
        half = s // middle
        pure = leads & (last < (half + 1) * middle)
        put(half * per_half + filled[half], s, last, 1, pure)
        filled[half] = filled[half] + count(pure)
        if half == 0:
            mixed.append((s, last, 1, leads & (last >= middle)))
        yield
    waiting, odd = [jnp.int32(0), jnp.int32(0)], [jnp.int32(0), jnp.int32(0)]
    for s in range(slots):
        half = s // middle
        second = alone[s] & (odd[half] == 1)
        put(half * per_half + filled[half], waiting[half], s, 0, second)
        filled[half] = filled[half] + count(second)
        odd[half] = jnp.where(alone[s], 1 - odd[half], odd[half])
        waiting[half] = jnp.where(alone[s], s, waiting[half])
        yield
    mixed.append((waiting[0], waiting[1], 0, odd[0] == 1))
    for low, high, coupled, really in mixed:
        room = filled[0] < per_half
        unit = jnp.where(room, filled[0], per_half + filled[1])
        put(unit, jnp.where(room, low, high), jnp.where(room, high, low), coupled, really)
        filled[0] = filled[0] + count(really & room)
        filled[1] = filled[1] + count(really & jnp.logical_not(room))
        yield


def pack_kernel(
    per_half, rows_ref, cols_ref, counts_ref, down_ref, up_ref,
    out_ref, order_ref, flags_ref, whole, first_a, last_a, first_b, last_b, sems,
):
    slots, owners = cols_ref.shape[2], counts_ref.shape[2]
    places, units, rows = out_ref.shape[0], 2 * per_half, whole.shape[1]
    pieces = sems.shape[1]
    copies = []
    for which, x_ref in ((0, down_ref), (1, up_ref)):
        for piece in range(pieces):
            part = pl.ds(piece * (rows // pieces), rows // pieces)
            copy = pltpu.make_async_copy(
                x_ref.at[0, 0, part], whole.at[which, part], sems.at[which, piece]
            )
            copy.start()
            copies.append(copy)
    steps = [
        order_units(cols_ref, counts_ref, which, slots, per_half, order_ref, flags_ref, *tables)
        for which, tables in enumerate(((first_a, last_a), (first_b, last_b)))
    ]
    for _ in itertools.zip_longest(*steps):
        pass
    used = [unit_place(unit, per_half, owners) for unit in range(units)]
    for place in range(places):
        if place not in used:
            out_ref[place] = jnp.zeros(out_ref.shape[1:], out_ref.dtype)
    for which in range(2):
        for copy in copies[which * pieces : (which + 1) * pieces]:
            copy.wait()
        for i in range(2 * units):
            row = rows_ref[0, which, jnp.maximum(order_ref[which, i], 0)]
            at = pl.multiple_of(row * TILE, TILE)
            out_ref[used[i // 2], which, i % 2] = whole[which, :, pl.ds(at, TILE)]


def pack(x_down, x_up, tile_rows, tile_cols, counts, per_half, places):
    rows, units = x_down.shape[2], 2 * per_half
    smem = pl.BlockSpec(memory_space=pltpu.SMEM)
    vmem = pl.BlockSpec(memory_space=pltpu.VMEM)
    hbm = pl.BlockSpec(memory_space=pl.ANY)
    return pl.pallas_call(
        functools.partial(pack_kernel, per_half),
        out_shape=[
            jax.ShapeDtypeStruct((places, 2, 2, rows, TILE), x_down.dtype),
            jax.ShapeDtypeStruct((2, 2 * units + 2), jnp.int32),
            jax.ShapeDtypeStruct((2, 2 * units + 2), jnp.int32),
        ],
        in_specs=[smem, smem, smem, hbm, hbm],
        out_specs=[vmem, smem, smem],
        scratch_shapes=[
            pltpu.VMEM((2,) + x_down.shape[2:], x_down.dtype),
            *[pltpu.SMEM((COLUMNS + 1,), jnp.int32)] * 4,
            pltpu.SemaphoreType.DMA((2, COPIES)),
        ],
        cost_estimate=pl.CostEstimate(
            flops=0, bytes_accessed=4 * x_down.size + 16 * units * rows * TILE, transcendentals=0
        ),
    )(tile_rows, tile_cols, counts, x_down, x_up)


def swapped(array, apart):
    size = lax.axis_size("fsdp")
    return lax.ppermute(array, "fsdp", [(i, i ^ apart) for i in range(size)])


def near_at(slot, per_owner):
    owner = slot // per_owner
    other = jnp.where(owner % CORES == lax.axis_index("fsdp") % CORES, 0, per_owner)
    return other + slot - owner * per_owner


def far_kernel(per_half, order_ref, near_ref, out_ref):
    per_owner, owners = near_ref.shape[1] // CORES, 2 * CORES
    unit = unit_here(per_half, owners)
    asker = jnp.where(unit < per_half, unit + per_half, unit - per_half)
    for which in range(2):
        slot = jnp.maximum(order_ref[which, 2 * asker + 1], 0)
        out_ref[which] = near_ref[which, near_at(slot, per_owner)]


def far_weights(near, order, per_half):
    vmem = pl.BlockSpec(memory_space=pltpu.VMEM)
    return pl.pallas_call(
        functools.partial(far_kernel, per_half),
        out_shape=jax.ShapeDtypeStruct(near.shape[:1] + near.shape[2:], near.dtype),
        in_specs=[pl.BlockSpec(memory_space=pltpu.SMEM), vmem],
        out_specs=vmem,
        compiler_params=IN_VMEM,
        cost_estimate=pl.CostEstimate(flops=0, bytes_accessed=300_000, transcendentals=0),
    )(order, near)


def dot(a, b, over_a, over_b):
    return lax.dot_general(
        a, b, (((over_a,), (over_b,)), ((), ())), preferred_element_type=jnp.float32
    )


def grads_kernel(
    which, per_half, owners, loss_scale, order_ref, flags_ref, x_ref, near_ref, far_ref, out_ref,
    w_unit, first_sum, second_sum,
):
    sources, _, _, rows, _ = x_ref.shape
    per_owner = near_ref.shape[1] // CORES
    unit = unit_here(per_half, owners)
    half = lax.axis_index("fsdp") // CORES
    for i in range(2):
        slot = jnp.maximum(order_ref[which, 2 * unit + i], 0)
        near = slot // per_owner // CORES == half

        @pl.when(near)
        def _():
            w_unit[i] = near_ref[which, near_at(slot, per_owner)]

        @pl.when(jnp.logical_not(near))
        def _():
            w_unit[i] = far_ref[which]

    together = min(SOURCES_AT_ONCE, sources)
    steps = sources // together
    if steps > 1:
        first_sum[...] = jnp.zeros_like(first_sum)
        second_sum[...] = jnp.zeros_like(second_sum)

    def sum_up(total_ref, where, term):
        total_ref[where] = total_ref[where] + term if steps > 1 else term

    coupled = flags_ref[which, 2 * unit] == 1

    def read(step):
        at = step * together
        return [
            x_ref[pl.ds(at, together), which, i].reshape(together * rows, TILE) for i in range(2)
        ]

    @pl.when(coupled)
    def _():
        def go(step, carry):
            xs = jnp.concatenate(read(step), axis=1)
            firsts = jnp.concatenate([w_unit[0, 0], w_unit[1, 0]], axis=0)
            seconds = jnp.concatenate([w_unit[0, 1], w_unit[1, 1]], axis=1)
            value, slope = gelu_pair(dot(xs, firsts, 1, 0))
            active = value.astype(jnp.bfloat16)
            delta = dot(active, seconds, 1, 0)
            cotangent = (loss_scale * (xs.astype(jnp.float32) + delta)).astype(jnp.bfloat16)
            grad_act = dot(cotangent, seconds, 1, 1)
            grad_pre = (grad_act * slope).astype(jnp.bfloat16)
            sum_up(first_sum, ..., dot(xs, grad_pre, 0, 0))
            sum_up(second_sum, ..., dot(active, cotangent, 0, 0))
            return carry

        lax.fori_loop(0, steps, go, 0, unroll=min(steps, 4))

    @pl.when(jnp.logical_not(coupled))
    def _():
        def go(step, carry):
            for i, x in enumerate(read(step)):
                across = slice(i * TILE, (i + 1) * TILE)
                value, slope = gelu_pair(dot(x, w_unit[i, 0], 1, 0))
                active = value.astype(jnp.bfloat16)
                delta = dot(active, w_unit[i, 1], 1, 0)
                cotangent = (loss_scale * (x.astype(jnp.float32) + delta)).astype(jnp.bfloat16)
                grad_act = dot(cotangent, w_unit[i, 1], 1, 1)
                grad_pre = (grad_act * slope).astype(jnp.bfloat16)
                sum_up(first_sum, (across, slice(None)), dot(x, grad_pre, 0, 0))
                sum_up(second_sum, (slice(None), across), dot(active, cotangent, 0, 0))
            return carry

        lax.fori_loop(0, steps, go, 0, unroll=min(steps, 4))

    for i in range(2):
        across = slice(i * TILE, (i + 1) * TILE)
        out_ref[i, 0] = first_sum[across, :].astype(out_ref.dtype)
        out_ref[i, 1] = second_sum[:, across].astype(out_ref.dtype)


def unit_grads(which, blocks, near, far, order, flags, per_half, owners, loss_scale, dtype):
    sources, _, _, rows, _ = blocks.shape
    smem = pl.BlockSpec(memory_space=pltpu.SMEM)
    vmem = pl.BlockSpec(memory_space=pltpu.VMEM)
    return pl.pallas_call(
        functools.partial(grads_kernel, which, per_half, owners, loss_scale),
        out_shape=jax.ShapeDtypeStruct((2, 2, TILE, TILE), dtype),
        in_specs=[smem, smem, vmem, vmem, vmem],
        out_specs=vmem,
        scratch_shapes=[
            pltpu.VMEM((2, 2, TILE, TILE), jnp.bfloat16),
            pltpu.VMEM((2 * TILE, TILE), jnp.float32),
            pltpu.VMEM((TILE, 2 * TILE), jnp.float32),
        ],
        compiler_params=IN_VMEM,
        cost_estimate=pl.CostEstimate(
            flops=20 * sources * rows * TILE * TILE,
            bytes_accessed=4 * sources * rows * TILE,
            transcendentals=2 * sources * rows * TILE,
        ),
    )(order, flags, blocks, near, far)


def add_kernel(own_ref, arrived_ref, out_ref):
    out_ref[...] = (own_ref[...] + arrived_ref[...].astype(jnp.float32)).astype(out_ref.dtype)


def add(own, arrived):
    vmem = pl.BlockSpec(memory_space=pltpu.VMEM)
    return pl.pallas_call(
        add_kernel,
        out_shape=jax.ShapeDtypeStruct(own.shape, jnp.bfloat16),
        in_specs=[vmem, vmem],
        out_specs=vmem,
        compiler_params=IN_VMEM,
        cost_estimate=pl.CostEstimate(flops=own.size, bytes_accessed=900_000, transcendentals=0),
    )(own, arrived)


def hand_round(mine):
    replicas = lax.axis_size("dp")
    near = jnp.concatenate(
        [mine]
        + [
            lax.ppermute(mine, "dp", [(i, (i + by) % replicas) for i in range(replicas)])
            for by in range(1, replicas)
        ],
        axis=0,
    )
    return jnp.concatenate([near, swapped(near[1::2], CORES)], axis=0)


def place_kernel(per_half, order_ref, counts_ref, same_ref, other_ref, out_ref, zeros, sems, zero_sems):
    owner, replicas = lax.axis_index("fsdp"), same_ref.shape[0] // 3
    per_owner = out_ref.shape[0]
    zeros[...] = jnp.zeros_like(zeros)

    def each(act):
        for i in range(4 * per_half):
            at = order_ref[0, i] - owner * per_owner
            mine = (at >= 0) & (at < per_owner)
            half, spot = i // 2 // per_half, i // 2 % per_half
            by = (lax.axis_index("dp") - spot // CORES + replicas) % replicas
            held = jnp.where(owner // CORES == half, 2 * by + i % 2, 2 * replicas + by)
            near = owner % CORES == spot % CORES
            for grads_ref, where in ((same_ref, near), (other_ref, jnp.logical_not(near))):

                @pl.when(mine & where)
                def _():
                    act(
                        pltpu.make_async_copy(
                            grads_ref.at[held], out_ref.at[at], sems.at[i]
                        )
                    )

        for slot in range(per_owner):

            @pl.when(counts_ref[0, 0, owner] <= slot)
            def _():
                act(pltpu.make_async_copy(zeros, out_ref.at[slot], zero_sems.at[slot]))

    each(lambda copy: copy.start())
    each(lambda copy: copy.wait())


def place(same, other, order, counts, per_half, per_owner):
    smem = pl.BlockSpec(memory_space=pltpu.SMEM)
    hbm = pl.BlockSpec(memory_space=pl.ANY)
    return pl.pallas_call(
        functools.partial(place_kernel, per_half),
        out_shape=jax.ShapeDtypeStruct((per_owner,) + same.shape[1:], same.dtype),
        in_specs=[smem, smem, hbm, hbm],
        out_specs=hbm,
        scratch_shapes=[
            pltpu.VMEM(same.shape[1:], same.dtype),
            pltpu.SemaphoreType.DMA((4 * per_half,)),
            pltpu.SemaphoreType.DMA((per_owner,)),
        ],
        compiler_params=IN_VMEM,
        cost_estimate=pl.CostEstimate(flops=0, bytes_accessed=1_000_000, transcendentals=0),
    )(order, counts, same, other)


def body(x_down, x_up, w_tiles, tile_rows, tile_cols, counts):
    rows_here = x_down.shape[2]
    slots, owners = tile_cols.shape[2], counts.shape[2]
    per_half = (live_total(slots, owners) // 2 + 1) // 2
    places = lax.axis_size("dp") * lax.axis_size("fsdp")
    sections = lax.axis_size("section")
    across = [(i, (i + sections // 2) % sections) for i in range(sections)]
    loss_scale = float(2 * rows_here * places) ** (-0.5)

    packed, order, flags = pack(x_down, x_up, tile_rows, tile_cols, counts, per_half, places)
    blocks = lax.all_to_all(packed, PLANE, split_axis=0, concat_axis=0, tiled=True)
    near = jnp.concatenate([w_tiles[0], swapped(w_tiles[0], 1)], axis=1)
    far = swapped(far_weights(near, order, per_half), CORES)
    grads = functools.partial(
        unit_grads, blocks=blocks, near=near, far=far, order=order, flags=flags,
        per_half=per_half, owners=owners, loss_scale=loss_scale,
    )
    arrived = lax.ppermute(grads(1, dtype=jnp.bfloat16), "section", across)
    mine = add(grads(0, dtype=jnp.float32), arrived)
    same = hand_round(mine)
    other = swapped(same, 1)
    return place(same, other, order, counts, per_half, slots // owners)[None]


def solution(mesh):
    in_specs = (
        P("section", "dp", "fsdp", None),
        P("section", "dp", "fsdp", None),
        P("section", None, "fsdp", None, None, None),
        P("section", None, None),
        P("section", None, None),
        P("section", None, None),
    )
    out_specs = P("section", "fsdp", None, None, None)
    return jax.shard_map(body, mesh=mesh, in_specs=in_specs, out_specs=out_specs, check_vma=False)
```

profile of v0, /device:TPU:0, one launch (start us, length us, event | category | flops | bytes accessed | tf_op | source)
XLA Modules:
  0.0 50.4 jit_solution(6081833118814276755)
XLA Ops:
  0.0 0.5 collective-permute-start
  0.5 3.7 %shard_map.64 = (bf16[8,2,2,128,128]{4,3,2,1,0:T(8,128)(2,1)}, s32[2,18]{1,0:T(2,128)}, s32[2,18]{1,0:T(2,128)}) custom-call(s32[1,2,20]{2,1,0:T(2,128)} %rows_ref.1, s32[1,2,20]{2,1,0:T(2,128)} %cols_ref.1, s32[1,2,4]{2,1,0:T(2,128)} %counts_ref.3, bf16[1,1,128,6144]{3,2,1,0:T(8,128)(2,1)} %down_ref.1, bf16[1,1,128,6144]{3,2,1,0:T(8,128)(2,1)} %up_ref.1), custom_call_target="tpu_custom_call" | custom-call | bytes 5242880 | tf_op jit(solution)/shard_map/pallas_call | solution.py:148
  4.2 0.0 copy-start.3
  4.2 5.0 %all-to-all-start = ((bf16[8,2,2,128,128]{4,3,2,1,0:T(8,128)(2,1)}), bf16[8,2,2,128,128]{4,3,2,1,0:T(8,128)(2,1)S(1)}, u32[]{:S(2)}, u32[]{:S(2)}) async-start(bf16[8,2,2,128,128]{4,3,2,1,0:T(8,128)(2,1)} %get-tuple-element.10), calls=%async_computation | async-start | bytes 2097152 | tf_op jit(solution)/shard_map/all_to_all | solution.py:397
  9.2 0.0 copy-start
  9.2 0.0 collective-permute-done
  9.2 0.0 copy-done.3
  9.2 1.2 %pad_maximum_fusion.near_ref = bf16[2,10,2,128,128]{4,3,2,1,0:T(8,128)(2,1)S(1)} fusion(bf16[2,5,2,128,128]{4,3,2,1,0:T(8,128)(2,1)} %collective-permute-done, bf16[2,5,2,128,128]{4,3,2,1,0:T(8,128)(2,1)S(1)} %bitcast.3), kind=kLoop, calls=%fused_computation | loop fusion | flops 655360 | bytes 2621440 | tf_op jit(solution)/shard_map/concatenate | solution.py:398
  10.4 0.0 copy-start.2
  10.4 0.0 copy-done
  10.4 0.6 %shard_map.65 = bf16[2,2,128,128]{3,2,1,0:T(8,128)(2,1)S(1)} custom-call(s32[2,18]{1,0:T(2,128)S(1)} %copy-done, bf16[2,10,2,128,128]{4,3,2,1,0:T(8,128)(2,1)S(1)} %pad_maximum_fusion.near_ref), custom_call_target="tpu_custom_call" | custom-call | bytes 300000 | tf_op jit(solution)/shard_map/pallas_call | solution.py:190
  11.0 2.1 %collective-permute-start.1 = (bf16[2,2,128,128]{3,2,1,0:T(8,128)(2,1)S(1)}, bf16[2,2,128,128]{3,2,1,0:T(8,128)(2,1)S(1)}, u32[]{:S(2)}, u32[]{:S(2)}) collective-permute-start(bf16[2,2,128,128]{3,2,1,0:T(8,128)(2,1)S(1)} %shard_map.65), channel_id=1, source_target_pairs={{0,2},{1,3},{2,0},{3,1},{4,6},{5,7},{6,4},{7,5},{8,10},{9,11},{10,... | collective-permute-start | bytes 393224 | tf_op jit(solution)/shard_map/ppermute | solution.py:170
  13.1 13.3 %collective-permute-done.1.far_ref = bf16[2,2,128,128]{3,2,1,0:T(8,128)(2,1)S(1)} collective-permute-done((bf16[2,2,128,128]{3,2,1,0:T(8,128)(2,1)S(1)}, bf16[2,2,128,128]{3,2,1,0:T(8,128)(2,1)S(1)}, u32[]{:S(2)}, u32[]{:S(2)}) %collective-permute-start.1) | collective-permute-done | bytes 131104 | tf_op jit(solution)/shard_map/ppermute | solution.py:170
  26.5 0.0 all-to-all-done.x_ref
  26.5 0.0 copy-done.2
  26.5 2.0 %shard_map.67 = bf16[2,2,128,128]{3,2,1,0:T(8,128)(2,1)S(1)} custom-call(s32[2,18]{1,0:T(2,128)S(1)} %copy-done, s32[2,18]{1,0:T(2,128)S(1)} %copy-done.2, bf16[8,2,2,128,128]{4,3,2,1,0:T(8,128)(2,1)S(1)} %all-to-all-done.x_ref, bf16[2,10,2,128,128]{4,3,2,1,0:T(8,128)(2,1)S(1)} %pad_maximum_fusion.near_ref, ...), custom_call_target="tpu_custom_call" | custom-call | flops 335544320 | bytes 524288 | tf_op jit(solution)/shard_map/pallas_call | solution.py:288
  28.5 2.3 %collective-permute-start.2 = (bf16[2,2,128,128]{3,2,1,0:T(8,128)(2,1)S(1)}, bf16[2,2,128,128]{3,2,1,0:T(8,128)(2,1)S(1)}, u32[]{:S(2)}, u32[]{:S(2)}) collective-permute-start(bf16[2,2,128,128]{3,2,1,0:T(8,128)(2,1)S(1)} %shard_map.67), channel_id=1, source_target_pairs={{0,16},{8,24},{16,0},{24,8},{1,17},{9,25},{17,1},{25,9},{2,18},{10... | collective-permute-start | bytes 393224 | tf_op jit(solution)/shard_map/ppermute | solution.py:404
  30.8 1.7 %shard_map.66.own_ref = f32[2,2,128,128]{3,2,1,0:T(8,128)S(1)} custom-call(s32[2,18]{1,0:T(2,128)S(1)} %copy-done, s32[2,18]{1,0:T(2,128)S(1)} %copy-done.2, bf16[8,2,2,128,128]{4,3,2,1,0:T(8,128)(2,1)S(1)} %all-to-all-done.x_ref, bf16[2,10,2,128,128]{4,3,2,1,0:T(8,128)(2,1)S(1)} %pad_maximum_fusion.near_ref, ...), custom_call_target="tpu_custom_call" | custom-call | flops 335544320 | bytes 524288 | tf_op jit(solution)/shard_map/pallas_call | solution.py:288
  32.5 0.0 copy-start.1
  32.5 4.5 %collective-permute-done.2.arrived_ref = bf16[2,2,128,128]{3,2,1,0:T(8,128)(2,1)S(1)} collective-permute-done((bf16[2,2,128,128]{3,2,1,0:T(8,128)(2,1)S(1)}, bf16[2,2,128,128]{3,2,1,0:T(8,128)(2,1)S(1)}, u32[]{:S(2)}, u32[]{:S(2)}) %collective-permute-start.2) | collective-permute-done | bytes 131104 | tf_op jit(solution)/shard_map/ppermute | solution.py:404
  37.0 1.5 %collective-permute-start.3 = (bf16[2,2,128,128]{3,2,1,0:T(8,128)(2,1)S(1)}, bf16[2,2,128,128]{3,2,1,0:T(8,128)(2,1)S(1)}, u32[]{:S(2)}, u32[]{:S(2)}) collective-permute-start(bf16[2,2,128,128]{3,2,1,0:T(8,128)(2,1)S(1)} %shard_map.68), channel_id=1, source_target_pairs={{0,4},{4,0},{1,5},{5,1},{2,6},{6,2},{3,7},{7,3},{8,12},{12,8},{9,1... | collective-permute-start | bytes 393224 | tf_op jit(solution)/shard_map/ppermute | solution.py:328
  38.5 3.5 %collective-permute-done.3 = bf16[2,2,128,128]{3,2,1,0:T(8,128)(2,1)S(1)} collective-permute-done((bf16[2,2,128,128]{3,2,1,0:T(8,128)(2,1)S(1)}, bf16[2,2,128,128]{3,2,1,0:T(8,128)(2,1)S(1)}, u32[]{:S(2)}, u32[]{:S(2)}) %collective-permute-start.3) | collective-permute-done | bytes 131104 | tf_op jit(solution)/shard_map/ppermute | solution.py:328
  42.1 1.0 %collective-permute-start.4 = (bf16[2,2,128,128]{3,2,1,0:T(8,128)(2,1)S(1)}, bf16[2,2,128,128]{3,2,1,0:T(8,128)(2,1)S(1)}, u32[]{:S(2)}, u32[]{:S(2)}) collective-permute-start(bf16[2,2,128,128]{3,2,1,0:T(8,128)(2,1)S(1)} %slice.3), channel_id=1, source_target_pairs={{0,2},{1,3},{2,0},{3,1},{4,6},{5,7},{6,4},{7,5},{8,10},{9,11},{10,... | collective-permute-start | bytes 393224 | tf_op jit(solution)/shard_map/ppermute | solution.py:170
  43.1 4.0 %collective-permute-done.4 = bf16[2,2,128,128]{3,2,1,0:T(8,128)(2,1)S(1)} collective-permute-done((bf16[2,2,128,128]{3,2,1,0:T(8,128)(2,1)S(1)}, bf16[2,2,128,128]{3,2,1,0:T(8,128)(2,1)S(1)}, u32[]{:S(2)}, u32[]{:S(2)}) %collective-permute-start.4) | collective-permute-done | bytes 131104 | tf_op jit(solution)/shard_map/ppermute | solution.py:170
  47.2 0.1 collective-permute-start.5
  47.2 1.7 %collective-permute-done.5.other_ref = bf16[6,2,128,128]{3,2,1,0:T(8,128)(2,1)S(1)} collective-permute-done((bf16[6,2,128,128]{3,2,1,0:T(8,128)(2,1)S(1)}, bf16[6,2,128,128]{3,2,1,0:T(8,128)(2,1)S(1)}, u32[]{:S(2)}, u32[]{:S(2)}) %collective-permute-start.5) | collective-permute-done | bytes 393248 | tf_op jit(solution)/shard_map/ppermute | solution.py:170
  48.9 0.0 copy-done.1
  48.9 1.5 %shard_map.69 = bf16[5,2,128,128]{3,2,1,0:T(8,128)(2,1)} custom-call(s32[2,18]{1,0:T(2,128)S(1)} %copy-done, s32[1,2,4]{2,1,0:T(2,128)S(1)} %copy-done.1, bf16[6,2,128,128]{3,2,1,0:T(8,128)(2,1)S(1)} %pad_maximum_fusion.1.same_ref, bf16[6,2,128,128]{3,2,1,0:T(8,128)(2,1)S(1)} %collective-permute-done.5.other_ref), custom_call_target="tpu_custom_call" | custom-call | bytes 1000000 | tf_op jit(solution)/shard_map/pallas_call | solution.py:372
  (4 shorter events, 0.1 us)
Async XLA Ops:
  0.0 9.2 %collective-permute-start = (bf16[2,5,2,128,128]{4,3,2,1,0:T(8,128)(2,1)}, bf16[2,5,2,128,128]{4,3,2,1,0:T(8,128)(2,1)}, u32[]{:S(2)}, u32[]{:S(2)}) collective-permute-start(bf16[2,5,2,128,128]{4,3,2,1,0:T(8,128)(2,1)} %bitcast.2), channel_id=1, source_target_pairs={{0,1},{1,0},{2,3},{3,2},{4,5},{5,4},{6,7},{7,6},{8,9},{9,8},{10,11... | collective-permute-start | bytes 1966088 | tf_op jit(solution)/shard_map/ppermute | solution.py:170
  4.2 5.0 %copy-start.3 = (bf16[1,2,5,2,128,128]{5,4,3,2,1,0:T(8,128)(2,1)S(1)}, bf16[1,2,5,2,128,128]{5,4,3,2,1,0:T(8,128)(2,1)}, u32[]{:S(2)}) copy-start(bf16[1,2,5,2,128,128]{5,4,3,2,1,0:T(8,128)(2,1)} %param.8) | copy-start | bytes 1966084
  4.2 22.3 %all-to-all-start = ((bf16[8,2,2,128,128]{4,3,2,1,0:T(8,128)(2,1)}), bf16[8,2,2,128,128]{4,3,2,1,0:T(8,128)(2,1)S(1)}, u32[]{:S(2)}, u32[]{:S(2)}) async-start(bf16[8,2,2,128,128]{4,3,2,1,0:T(8,128)(2,1)} %get-tuple-element.10), calls=%async_computation | async-start | bytes 2097152 | tf_op jit(solution)/shard_map/all_to_all | solution.py:397
  9.2 1.2 %copy-start = (s32[2,18]{1,0:T(2,128)S(1)}, s32[2,18]{1,0:T(2,128)}, u32[]{:S(2)}) copy-start(s32[2,18]{1,0:T(2,128)} %get-tuple-element.8.order_ref) | copy-start | bytes 436
  10.4 16.0 %copy-start.2 = (s32[2,18]{1,0:T(2,128)S(1)}, s32[2,18]{1,0:T(2,128)}, u32[]{:S(2)}) copy-start(s32[2,18]{1,0:T(2,128)} %get-tuple-element.9.flags_ref) | copy-start | bytes 436
  11.0 15.4 %collective-permute-start.1 = (bf16[2,2,128,128]{3,2,1,0:T(8,128)(2,1)S(1)}, bf16[2,2,128,128]{3,2,1,0:T(8,128)(2,1)S(1)}, u32[]{:S(2)}, u32[]{:S(2)}) collective-permute-start(bf16[2,2,128,128]{3,2,1,0:T(8,128)(2,1)S(1)} %shard_map.65), channel_id=1, source_target_pairs={{0,2},{1,3},{2,0},{3,1},{4,6},{5,7},{6,4},{7,5},{8,10},{9,11},{10,... | collective-permute-start | bytes 393224 | tf_op jit(solution)/shard_map/ppermute | solution.py:170
  28.5 8.5 %collective-permute-start.2 = (bf16[2,2,128,128]{3,2,1,0:T(8,128)(2,1)S(1)}, bf16[2,2,128,128]{3,2,1,0:T(8,128)(2,1)S(1)}, u32[]{:S(2)}, u32[]{:S(2)}) collective-permute-start(bf16[2,2,128,128]{3,2,1,0:T(8,128)(2,1)S(1)} %shard_map.67), channel_id=1, source_target_pairs={{0,16},{8,24},{16,0},{24,8},{1,17},{9,25},{17,1},{25,9},{2,18},{10... | collective-permute-start | bytes 393224 | tf_op jit(solution)/shard_map/ppermute | solution.py:404
  32.5 16.4 %copy-start.1 = (s32[1,2,4]{2,1,0:T(2,128)S(1)}, s32[1,2,4]{2,1,0:T(2,128)}, u32[]{:S(2)}) copy-start(s32[1,2,4]{2,1,0:T(2,128)} %counts_ref.3) | copy-start | bytes 100
  37.0 5.0 %collective-permute-start.3 = (bf16[2,2,128,128]{3,2,1,0:T(8,128)(2,1)S(1)}, bf16[2,2,128,128]{3,2,1,0:T(8,128)(2,1)S(1)}, u32[]{:S(2)}, u32[]{:S(2)}) collective-permute-start(bf16[2,2,128,128]{3,2,1,0:T(8,128)(2,1)S(1)} %shard_map.68), channel_id=1, source_target_pairs={{0,4},{4,0},{1,5},{5,1},{2,6},{6,2},{3,7},{7,3},{8,12},{12,8},{9,1... | collective-permute-start | bytes 393224 | tf_op jit(solution)/shard_map/ppermute | solution.py:328
  42.1 5.0 %collective-permute-start.4 = (bf16[2,2,128,128]{3,2,1,0:T(8,128)(2,1)S(1)}, bf16[2,2,128,128]{3,2,1,0:T(8,128)(2,1)S(1)}, u32[]{:S(2)}, u32[]{:S(2)}) collective-permute-start(bf16[2,2,128,128]{3,2,1,0:T(8,128)(2,1)S(1)} %slice.3), channel_id=1, source_target_pairs={{0,2},{1,3},{2,0},{3,1},{4,6},{5,7},{6,4},{7,5},{8,10},{9,11},{10,... | collective-permute-start | bytes 393224 | tf_op jit(solution)/shard_map/ppermute | solution.py:170
  47.2 1.8 %collective-permute-start.5 = (bf16[6,2,128,128]{3,2,1,0:T(8,128)(2,1)S(1)}, bf16[6,2,128,128]{3,2,1,0:T(8,128)(2,1)S(1)}, u32[]{:S(2)}, u32[]{:S(2)}) collective-permute-start(bf16[6,2,128,128]{3,2,1,0:T(8,128)(2,1)S(1)} %pad_maximum_fusion.1.same_ref), channel_id=1, source_target_pairs={{0,1},{1,0},{2,3},{3,2},{4,5},{5,4},{6,7},{7,6},{8,9},{9,8},{10,11... | collective-permute-start | bytes 1179656 | tf_op jit(solution)/shard_map/ppermute | solution.py:170
where the time goes:
time: 50.7 us; the launch traced here: 50.4 us
  waiting for transfers between devices  27 us (53%)
  starting transfers between devices  12.5 us (25%)
  Pallas kernels  9.53 us (19%)
  other arithmetic  1.28 us (3%)
    ppermute x4, waiting for transfers between devices, swapped(): return lax.ppermute(array, 'fsdp', [(i, i ^ apart) for i in range(size)])  19 us
    all_to_all x1, starting transfers between devices, body(): lax.all_to_all(packed, PLANE, split_axis=0, concat_axis=0, tiled=True)  4.98 us
    ppermute x1, waiting for transfers between devices, body(): arrived = lax.ppermute(grads(1, dtype=jnp.bfloat16), 'section', across)  4.45 us
    pallas_call x1, Pallas kernels, pack(): pl.pallas_call(functools.partial(pack_kernel, per_half), out_shape=[jax.S...  3.74 us
    pallas_call x2, Pallas kernels, unit_grads(): pl.pallas_call(functools.partial(grads_kernel, which, per_half, owners, l...  3.68 us
    ppermute x4, starting transfers between devices, swapped(): return lax.ppermute(array, 'fsdp', [(i, i ^ apart) for i in range(size)])  3.64 us
    ppermute x1, waiting for transfers between devices, hand_round(): lax.ppermute(mine, 'dp', [(i, (i + by) % replicas) for i in range(replica...  3.5 us
    ppermute x1, starting transfers between devices, body(): arrived = lax.ppermute(grads(1, dtype=jnp.bfloat16), 'section', across)  2.34 us
  transfers between devices with their start and end apart: 7, of which 5 were waited for; matrix products, arithmetic and copies ran while one was open for 2% of the time, Pallas kernels for 12%

commit v1 on v0

--- a/solution.py
+++ b/solution.py
@@ -333,37 +333,38 @@
     return jnp.concatenate([near, swapped(near[1::2], CORES)], axis=0)
 
 
-def place_kernel(per_half, order_ref, counts_ref, same_ref, other_ref, out_ref, zeros, sems, zero_sems):
+def place_kernel(
+    per_half, order_ref, counts_ref, same_ref, other_ref, out_ref, zeros, source_ref, sems
+):
     owner, replicas = lax.axis_index("fsdp"), same_ref.shape[0] // 3
     per_owner = out_ref.shape[0]
     zeros[...] = jnp.zeros_like(zeros)
-
-    def each(act):
-        for i in range(4 * per_half):
-            at = order_ref[0, i] - owner * per_owner
-            mine = (at >= 0) & (at < per_owner)
-            half, spot = i // 2 // per_half, i // 2 % per_half
-            by = (lax.axis_index("dp") - spot // CORES + replicas) % replicas
-            held = jnp.where(owner // CORES == half, 2 * by + i % 2, 2 * replicas + by)
-            near = owner % CORES == spot % CORES
-            for grads_ref, where in ((same_ref, near), (other_ref, jnp.logical_not(near))):
-
-                @pl.when(mine & where)
-                def _():
-                    act(
-                        pltpu.make_async_copy(
-                            grads_ref.at[held], out_ref.at[at], sems.at[i]
-                        )
-                    )
-
-        for slot in range(per_owner):
-
-            @pl.when(counts_ref[0, 0, owner] <= slot)
+    for slot in range(per_owner):
+        source_ref[slot] = 0
+    for i in range(4 * per_half):
+        at = order_ref[0, i] - owner * per_owner
+        mine = (at >= 0) & (at < per_owner)
+        half, spot = i // 2 // per_half, i // 2 % per_half
+        by = (lax.axis_index("dp") - spot // CORES + replicas) % replicas
+        held = jnp.where(owner // CORES == half, 2 * by + i % 2, 2 * replicas + by)
+        other = jnp.where(owner % CORES == spot % CORES, 0, 1)
+        source_ref[jnp.where(mine, at, per_owner)] = 2 * held + other
+    for slot in range(per_owner):
+        living, source = counts_ref[0, 0, owner] > slot, source_ref[slot]
+        for kind, grads_ref in enumerate((same_ref, other_ref)):
+
+            @pl.when(living & (source % 2 == kind))
             def _():
-                act(pltpu.make_async_copy(zeros, out_ref.at[slot], zero_sems.at[slot]))
-
-    each(lambda copy: copy.start())
-    each(lambda copy: copy.wait())
+                pltpu.make_async_copy(
+                    grads_ref.at[source // 2], out_ref.at[slot], sems.at[slot]
+                ).start()
+
+        @pl.when(jnp.logical_not(living))
+        def _():
+            pltpu.make_async_copy(zeros, out_ref.at[slot], sems.at[slot]).start()
+
+    for slot in range(per_owner):
+        pltpu.make_async_copy(zeros, out_ref.at[slot], sems.at[slot]).wait()
 
 
 def place(same, other, order, counts, per_half, per_owner):
@@ -376,7 +377,7 @@
         out_specs=hbm,
         scratch_shapes=[
             pltpu.VMEM(same.shape[1:], same.dtype),
-            pltpu.SemaphoreType.DMA((4 * per_half,)),
+            pltpu.SMEM((per_owner + 1,), jnp.int32),
             pltpu.SemaphoreType.DMA((per_owner,)),
         ],
         compiler_params=IN_VMEM,

time: 50.7 us -> 50.9 us (level)
  waiting for transfers between devices: 27 us -> 28 us
where the time goes in v1:
time: 50.9 us; the launch traced here: 50.7 us
  waiting for transfers between devices  28 us (55%)
  starting transfers between devices  12.1 us (24%)
  Pallas kernels  9.12 us (18%)
  other arithmetic  1.28 us (3%)
    ppermute x4, waiting for transfers between devices, swapped(): return lax.ppermute(array, 'fsdp', [(i, i ^ apart) for i in range(size)])  19.4 us
    all_to_all x1, starting transfers between devices, body(): lax.all_to_all(packed, PLANE, split_axis=0, concat_axis=0, tiled=True)  4.98 us
    ppermute x1, waiting for transfers between devices, body(): arrived = lax.ppermute(grads(1, dtype=jnp.bfloat16), 'section', across)  4.77 us
    ppermute x1, waiting for transfers between devices, hand_round(): lax.ppermute(mine, 'dp', [(i, (i + by) % replicas) for i in range(replica...  3.83 us
    pallas_call x1, Pallas kernels, pack(): pl.pallas_call(functools.partial(pack_kernel, per_half), out_shape=[jax.S...  3.74 us
    pallas_call x2, Pallas kernels, unit_grads(): pl.pallas_call(functools.partial(grads_kernel, which, per_half, owners, l...  3.37 us
    ppermute x4, starting transfers between devices, swapped(): return lax.ppermute(array, 'fsdp', [(i, i ^ apart) for i in range(size)])  3.27 us
    ppermute x1, starting transfers between devices, body(): arrived = lax.ppermute(grads(1, dtype=jnp.bfloat16), 'section', across)  2.65 us
  transfers between devices with their start and end apart: 7, of which 5 were waited for; matrix products, arithmetic and copies ran while one was open for 2% of the time, Pallas kernels for 12%

profile of v1, /device:TPU:0, one launch (start us, length us, event | category | flops | bytes accessed | tf_op | source)
XLA Modules:
  0.0 50.7 jit_solution(2417818609914644009)
XLA Ops:
  0.0 0.5 collective-permute-start
  0.5 3.7 %shard_map.64 = (bf16[8,2,2,128,128]{4,3,2,1,0:T(8,128)(2,1)}, s32[2,18]{1,0:T(2,128)}, s32[2,18]{1,0:T(2,128)}) custom-call(s32[1,2,20]{2,1,0:T(2,128)} %rows_ref.1, s32[1,2,20]{2,1,0:T(2,128)} %cols_ref.1, s32[1,2,4]{2,1,0:T(2,128)} %counts_ref.3, bf16[1,1,128,6144]{3,2,1,0:T(8,128)(2,1)} %down_ref.1, bf16[1,1,128,6144]{3,2,1,0:T(8,128)(2,1)} %up_ref.1), custom_call_target="tpu_custom_call" | custom-call | bytes 5242880 | tf_op jit(solution)/shard_map/pallas_call | solution.py:148
  4.2 0.0 copy-start.3
  4.2 5.0 %all-to-all-start = ((bf16[8,2,2,128,128]{4,3,2,1,0:T(8,128)(2,1)}), bf16[8,2,2,128,128]{4,3,2,1,0:T(8,128)(2,1)S(1)}, u32[]{:S(2)}, u32[]{:S(2)}) async-start(bf16[8,2,2,128,128]{4,3,2,1,0:T(8,128)(2,1)} %get-tuple-element.10), calls=%async_computation | async-start | bytes 2097152 | tf_op jit(solution)/shard_map/all_to_all | solution.py:398
  9.2 0.0 copy-start
  9.2 0.0 collective-permute-done
  9.2 0.0 copy-done.3
  9.2 1.2 %pad_maximum_fusion.near_ref = bf16[2,10,2,128,128]{4,3,2,1,0:T(8,128)(2,1)S(1)} fusion(bf16[2,5,2,128,128]{4,3,2,1,0:T(8,128)(2,1)} %collective-permute-done, bf16[2,5,2,128,128]{4,3,2,1,0:T(8,128)(2,1)S(1)} %bitcast.3), kind=kLoop, calls=%fused_computation | loop fusion | flops 655360 | bytes 2621440 | tf_op jit(solution)/shard_map/concatenate | solution.py:399
  10.4 0.0 copy-start.2
  10.4 0.0 copy-done
  10.4 0.6 %shard_map.65 = bf16[2,2,128,128]{3,2,1,0:T(8,128)(2,1)S(1)} custom-call(s32[2,18]{1,0:T(2,128)S(1)} %copy-done, bf16[2,10,2,128,128]{4,3,2,1,0:T(8,128)(2,1)S(1)} %pad_maximum_fusion.near_ref), custom_call_target="tpu_custom_call" | custom-call | bytes 300000 | tf_op jit(solution)/shard_map/pallas_call | solution.py:190
  11.0 2.1 %collective-permute-start.1 = (bf16[2,2,128,128]{3,2,1,0:T(8,128)(2,1)S(1)}, bf16[2,2,128,128]{3,2,1,0:T(8,128)(2,1)S(1)}, u32[]{:S(2)}, u32[]{:S(2)}) collective-permute-start(bf16[2,2,128,128]{3,2,1,0:T(8,128)(2,1)S(1)} %shard_map.65), channel_id=1, source_target_pairs={{0,2},{1,3},{2,0},{3,1},{4,6},{5,7},{6,4},{7,5},{8,10},{9,11},{10,... | collective-permute-start | bytes 393224 | tf_op jit(solution)/shard_map/ppermute | solution.py:170
  13.1 13.3 %collective-permute-done.1.far_ref = bf16[2,2,128,128]{3,2,1,0:T(8,128)(2,1)S(1)} collective-permute-done((bf16[2,2,128,128]{3,2,1,0:T(8,128)(2,1)S(1)}, bf16[2,2,128,128]{3,2,1,0:T(8,128)(2,1)S(1)}, u32[]{:S(2)}, u32[]{:S(2)}) %collective-permute-start.1) | collective-permute-done | bytes 131104 | tf_op jit(solution)/shard_map/ppermute | solution.py:170
  26.5 0.0 all-to-all-done.x_ref
  26.5 0.0 copy-done.2
  26.5 1.7 %shard_map.67 = bf16[2,2,128,128]{3,2,1,0:T(8,128)(2,1)S(1)} custom-call(s32[2,18]{1,0:T(2,128)S(1)} %copy-done, s32[2,18]{1,0:T(2,128)S(1)} %copy-done.2, bf16[8,2,2,128,128]{4,3,2,1,0:T(8,128)(2,1)S(1)} %all-to-all-done.x_ref, bf16[2,10,2,128,128]{4,3,2,1,0:T(8,128)(2,1)S(1)} %pad_maximum_fusion.near_ref, ...), custom_call_target="tpu_custom_call" | custom-call | flops 335544320 | bytes 524288 | tf_op jit(solution)/shard_map/pallas_call | solution.py:288
  28.2 2.7 %collective-permute-start.2 = (bf16[2,2,128,128]{3,2,1,0:T(8,128)(2,1)S(1)}, bf16[2,2,128,128]{3,2,1,0:T(8,128)(2,1)S(1)}, u32[]{:S(2)}, u32[]{:S(2)}) collective-permute-start(bf16[2,2,128,128]{3,2,1,0:T(8,128)(2,1)S(1)} %shard_map.67), channel_id=1, source_target_pairs={{0,16},{8,24},{16,0},{24,8},{1,17},{9,25},{17,1},{25,9},{2,18},{10... | collective-permute-start | bytes 393224 | tf_op jit(solution)/shard_map/ppermute | solution.py:405
  30.8 1.7 %shard_map.66.own_ref = f32[2,2,128,128]{3,2,1,0:T(8,128)S(1)} custom-call(s32[2,18]{1,0:T(2,128)S(1)} %copy-done, s32[2,18]{1,0:T(2,128)S(1)} %copy-done.2, bf16[8,2,2,128,128]{4,3,2,1,0:T(8,128)(2,1)S(1)} %all-to-all-done.x_ref, bf16[2,10,2,128,128]{4,3,2,1,0:T(8,128)(2,1)S(1)} %pad_maximum_fusion.near_ref, ...), custom_call_target="tpu_custom_call" | custom-call | flops 335544320 | bytes 524288 | tf_op jit(solution)/shard_map/pallas_call | solution.py:288
  32.5 0.0 copy-start.1
  32.5 4.8 %collective-permute-done.2.arrived_ref = bf16[2,2,128,128]{3,2,1,0:T(8,128)(2,1)S(1)} collective-permute-done((bf16[2,2,128,128]{3,2,1,0:T(8,128)(2,1)S(1)}, bf16[2,2,128,128]{3,2,1,0:T(8,128)(2,1)S(1)}, u32[]{:S(2)}, u32[]{:S(2)}) %collective-permute-start.2) | collective-permute-done | bytes 131104 | tf_op jit(solution)/shard_map/ppermute | solution.py:405
  37.3 1.2 %collective-permute-start.3 = (bf16[2,2,128,128]{3,2,1,0:T(8,128)(2,1)S(1)}, bf16[2,2,128,128]{3,2,1,0:T(8,128)(2,1)S(1)}, u32[]{:S(2)}, u32[]{:S(2)}) collective-permute-start(bf16[2,2,128,128]{3,2,1,0:T(8,128)(2,1)S(1)} %shard_map.68), channel_id=1, source_target_pairs={{0,4},{4,0},{1,5},{5,1},{2,6},{6,2},{3,7},{7,3},{8,12},{12,8},{9,1... | collective-permute-start | bytes 393224 | tf_op jit(solution)/shard_map/ppermute | solution.py:328
  38.5 3.8 %collective-permute-done.3 = bf16[2,2,128,128]{3,2,1,0:T(8,128)(2,1)S(1)} collective-permute-done((bf16[2,2,128,128]{3,2,1,0:T(8,128)(2,1)S(1)}, bf16[2,2,128,128]{3,2,1,0:T(8,128)(2,1)S(1)}, u32[]{:S(2)}, u32[]{:S(2)}) %collective-permute-start.3) | collective-permute-done | bytes 131104 | tf_op jit(solution)/shard_map/ppermute | solution.py:328
  42.4 0.7 %collective-permute-start.4 = (bf16[2,2,128,128]{3,2,1,0:T(8,128)(2,1)S(1)}, bf16[2,2,128,128]{3,2,1,0:T(8,128)(2,1)S(1)}, u32[]{:S(2)}, u32[]{:S(2)}) collective-permute-start(bf16[2,2,128,128]{3,2,1,0:T(8,128)(2,1)S(1)} %slice.3), channel_id=1, source_target_pairs={{0,2},{1,3},{2,0},{3,1},{4,6},{5,7},{6,4},{7,5},{8,10},{9,11},{10,... | collective-permute-start | bytes 393224 | tf_op jit(solution)/shard_map/ppermute | solution.py:170
  43.1 4.4 %collective-permute-done.4 = bf16[2,2,128,128]{3,2,1,0:T(8,128)(2,1)S(1)} collective-permute-done((bf16[2,2,128,128]{3,2,1,0:T(8,128)(2,1)S(1)}, bf16[2,2,128,128]{3,2,1,0:T(8,128)(2,1)S(1)}, u32[]{:S(2)}, u32[]{:S(2)}) %collective-permute-start.4) | collective-permute-done | bytes 131104 | tf_op jit(solution)/shard_map/ppermute | solution.py:170
  47.5 0.1 collective-permute-start.5
  47.6 1.7 %collective-permute-done.5.other_ref = bf16[6,2,128,128]{3,2,1,0:T(8,128)(2,1)S(1)} collective-permute-done((bf16[6,2,128,128]{3,2,1,0:T(8,128)(2,1)S(1)}, bf16[6,2,128,128]{3,2,1,0:T(8,128)(2,1)S(1)}, u32[]{:S(2)}, u32[]{:S(2)}) %collective-permute-start.5) | collective-permute-done | bytes 393248 | tf_op jit(solution)/shard_map/ppermute | solution.py:170
  49.3 0.0 copy-done.1
  49.3 1.4 %shard_map.69 = bf16[5,2,128,128]{3,2,1,0:T(8,128)(2,1)} custom-call(s32[2,18]{1,0:T(2,128)S(1)} %copy-done, s32[1,2,4]{2,1,0:T(2,128)S(1)} %copy-done.1, bf16[6,2,128,128]{3,2,1,0:T(8,128)(2,1)S(1)} %pad_maximum_fusion.1.same_ref, bf16[6,2,128,128]{3,2,1,0:T(8,128)(2,1)S(1)} %collective-permute-done.5.other_ref), custom_call_target="tpu_custom_call" | custom-call | bytes 1000000 | tf_op jit(solution)/shard_map/pallas_call | solution.py:373
  (4 shorter events, 0.1 us)
Async XLA Ops:
  0.0 9.2 %collective-permute-start = (bf16[2,5,2,128,128]{4,3,2,1,0:T(8,128)(2,1)}, bf16[2,5,2,128,128]{4,3,2,1,0:T(8,128)(2,1)}, u32[]{:S(2)}, u32[]{:S(2)}) collective-permute-start(bf16[2,5,2,128,128]{4,3,2,1,0:T(8,128)(2,1)} %bitcast.2), channel_id=1, source_target_pairs={{0,1},{1,0},{2,3},{3,2},{4,5},{5,4},{6,7},{7,6},{8,9},{9,8},{10,11... | collective-permute-start | bytes 1966088 | tf_op jit(solution)/shard_map/ppermute | solution.py:170
  4.2 5.0 %copy-start.3 = (bf16[1,2,5,2,128,128]{5,4,3,2,1,0:T(8,128)(2,1)S(1)}, bf16[1,2,5,2,128,128]{5,4,3,2,1,0:T(8,128)(2,1)}, u32[]{:S(2)}) copy-start(bf16[1,2,5,2,128,128]{5,4,3,2,1,0:T(8,128)(2,1)} %param.8) | copy-start | bytes 1966084
  4.2 22.3 %all-to-all-start = ((bf16[8,2,2,128,128]{4,3,2,1,0:T(8,128)(2,1)}), bf16[8,2,2,128,128]{4,3,2,1,0:T(8,128)(2,1)S(1)}, u32[]{:S(2)}, u32[]{:S(2)}) async-start(bf16[8,2,2,128,128]{4,3,2,1,0:T(8,128)(2,1)} %get-tuple-element.10), calls=%async_computation | async-start | bytes 2097152 | tf_op jit(solution)/shard_map/all_to_all | solution.py:398
  9.2 1.2 %copy-start = (s32[2,18]{1,0:T(2,128)S(1)}, s32[2,18]{1,0:T(2,128)}, u32[]{:S(2)}) copy-start(s32[2,18]{1,0:T(2,128)} %get-tuple-element.8.order_ref) | copy-start | bytes 436
  10.4 16.0 %copy-start.2 = (s32[2,18]{1,0:T(2,128)S(1)}, s32[2,18]{1,0:T(2,128)}, u32[]{:S(2)}) copy-start(s32[2,18]{1,0:T(2,128)} %get-tuple-element.9.flags_ref) | copy-start | bytes 436
  11.0 15.4 %collective-permute-start.1 = (bf16[2,2,128,128]{3,2,1,0:T(8,128)(2,1)S(1)}, bf16[2,2,128,128]{3,2,1,0:T(8,128)(2,1)S(1)}, u32[]{:S(2)}, u32[]{:S(2)}) collective-permute-start(bf16[2,2,128,128]{3,2,1,0:T(8,128)(2,1)S(1)} %shard_map.65), channel_id=1, source_target_pairs={{0,2},{1,3},{2,0},{3,1},{4,6},{5,7},{6,4},{7,5},{8,10},{9,11},{10,... | collective-permute-start | bytes 393224 | tf_op jit(solution)/shard_map/ppermute | solution.py:170
  28.2 9.1 %collective-permute-start.2 = (bf16[2,2,128,128]{3,2,1,0:T(8,128)(2,1)S(1)}, bf16[2,2,128,128]{3,2,1,0:T(8,128)(2,1)S(1)}, u32[]{:S(2)}, u32[]{:S(2)}) collective-permute-start(bf16[2,2,128,128]{3,2,1,0:T(8,128)(2,1)S(1)} %shard_map.67), channel_id=1, source_target_pairs={{0,16},{8,24},{16,0},{24,8},{1,17},{9,25},{17,1},{25,9},{2,18},{10... | collective-permute-start | bytes 393224 | tf_op jit(solution)/shard_map/ppermute | solution.py:405
  32.5 16.8 %copy-start.1 = (s32[1,2,4]{2,1,0:T(2,128)S(1)}, s32[1,2,4]{2,1,0:T(2,128)}, u32[]{:S(2)}) copy-start(s32[1,2,4]{2,1,0:T(2,128)} %counts_ref.3) | copy-start | bytes 100
  37.3 5.0 %collective-permute-start.3 = (bf16[2,2,128,128]{3,2,1,0:T(8,128)(2,1)S(1)}, bf16[2,2,128,128]{3,2,1,0:T(8,128)(2,1)S(1)}, u32[]{:S(2)}, u32[]{:S(2)}) collective-permute-start(bf16[2,2,128,128]{3,2,1,0:T(8,128)(2,1)S(1)} %shard_map.68), channel_id=1, source_target_pairs={{0,4},{4,0},{1,5},{5,1},{2,6},{6,2},{3,7},{7,3},{8,12},{12,8},{9,1... | collective-permute-start | bytes 393224 | tf_op jit(solution)/shard_map/ppermute | solution.py:328
  42.4 5.0 %collective-permute-start.4 = (bf16[2,2,128,128]{3,2,1,0:T(8,128)(2,1)S(1)}, bf16[2,2,128,128]{3,2,1,0:T(8,128)(2,1)S(1)}, u32[]{:S(2)}, u32[]{:S(2)}) collective-permute-start(bf16[2,2,128,128]{3,2,1,0:T(8,128)(2,1)S(1)} %slice.3), channel_id=1, source_target_pairs={{0,2},{1,3},{2,0},{3,1},{4,6},{5,7},{6,4},{7,5},{8,10},{9,11},{10,... | collective-permute-start | bytes 393224 | tf_op jit(solution)/shard_map/ppermute | solution.py:170
  47.5 1.8 %collective-permute-start.5 = (bf16[6,2,128,128]{3,2,1,0:T(8,128)(2,1)S(1)}, bf16[6,2,128,128]{3,2,1,0:T(8,128)(2,1)S(1)}, u32[]{:S(2)}, u32[]{:S(2)}) collective-permute-start(bf16[6,2,128,128]{3,2,1,0:T(8,128)(2,1)S(1)} %pad_maximum_fusion.1.same_ref), channel_id=1, source_target_pairs={{0,1},{1,0},{2,3},{3,2},{4,5},{5,4},{6,7},{7,6},{8,9},{9,8},{10,11... | collective-permute-start | bytes 1179656 | tf_op jit(solution)/shard_map/ppermute | solution.py:170

commit v2 on v1

--- a/solution.py
+++ b/solution.py
@@ -14,7 +14,7 @@
 SOURCES_AT_ONCE = 8
 COLUMNS = 192
 CORES = 2
-COPIES = 4
+COPIES = 1
 IN_VMEM = pltpu.CompilerParams(vmem_limit_bytes=16 * 1024 * 1024)
 
 tanh_scale = math.sqrt(2.0 / math.pi)

time: 50.9 us -> 50.7 us (level)
  waiting for transfers between devices: 28 us -> 26.7 us
  starting transfers between devices: 12.1 us -> 13.1 us
    ppermute x1, waiting for transfers between devices: 3.83 us -> 3.19 us  [hand_round(): lax.ppermute(mine, 'dp', [(i, (i + by) % replicas) for i in range(replica...]
    ppermute x1, starting transfers between devices: 1.21 us -> 1.85 us  [hand_round(): lax.ppermute(mine, 'dp', [(i, (i + by) % replicas) for i in range(replica...]
where the time goes in v2:
time: 50.7 us; the launch traced here: 50.4 us
  waiting for transfers between devices  26.7 us (53%)
  starting transfers between devices  13.1 us (26%)
  Pallas kernels  9.13 us (18%)
  other arithmetic  1.28 us (3%)
    ppermute x4, waiting for transfers between devices, swapped(): return lax.ppermute(array, 'fsdp', [(i, i ^ apart) for i in range(size)])  19 us
    all_to_all x1, starting transfers between devices, body(): lax.all_to_all(packed, PLANE, split_axis=0, concat_axis=0, tiled=True)  4.98 us
    ppermute x1, waiting for transfers between devices, body(): arrived = lax.ppermute(grads(1, dtype=jnp.bfloat16), 'section', across)  4.46 us
    pallas_call x1, Pallas kernels, pack(): pl.pallas_call(functools.partial(pack_kernel, per_half), out_shape=[jax.S...  3.74 us
    ppermute x4, starting transfers between devices, swapped(): return lax.ppermute(array, 'fsdp', [(i, i ^ apart) for i in range(size)])  3.64 us
    pallas_call x2, Pallas kernels, unit_grads(): pl.pallas_call(functools.partial(grads_kernel, which, per_half, owners, l...  3.37 us
    ppermute x1, waiting for transfers between devices, hand_round(): lax.ppermute(mine, 'dp', [(i, (i + by) % replicas) for i in range(replica...  3.19 us
    ppermute x1, starting transfers between devices, body(): arrived = lax.ppermute(grads(1, dtype=jnp.bfloat16), 'section', across)  2.65 us
  transfers between devices with their start and end apart: 7, of which 5 were waited for; matrix products, arithmetic and copies ran while one was open for 2% of the time, Pallas kernels for 12%

profile of v2, /device:TPU:0, one launch (start us, length us, event | category | flops | bytes accessed | tf_op | source)
XLA Modules:
  0.0 50.4 jit_solution(12728355563690567899)
XLA Ops:
  0.0 0.5 collective-permute-start
  0.5 3.7 %shard_map.64 = (bf16[8,2,2,128,128]{4,3,2,1,0:T(8,128)(2,1)}, s32[2,18]{1,0:T(2,128)}, s32[2,18]{1,0:T(2,128)}) custom-call(s32[1,2,20]{2,1,0:T(2,128)} %rows_ref.1, s32[1,2,20]{2,1,0:T(2,128)} %cols_ref.1, s32[1,2,4]{2,1,0:T(2,128)} %counts_ref.3, bf16[1,1,128,6144]{3,2,1,0:T(8,128)(2,1)} %down_ref.1, bf16[1,1,128,6144]{3,2,1,0:T(8,128)(2,1)} %up_ref.1), custom_call_target="tpu_custom_call" | custom-call | bytes 5242880 | tf_op jit(solution)/shard_map/pallas_call | solution.py:148
  4.2 0.0 copy-start.3
  4.2 5.0 %all-to-all-start = ((bf16[8,2,2,128,128]{4,3,2,1,0:T(8,128)(2,1)}), bf16[8,2,2,128,128]{4,3,2,1,0:T(8,128)(2,1)S(1)}, u32[]{:S(2)}, u32[]{:S(2)}) async-start(bf16[8,2,2,128,128]{4,3,2,1,0:T(8,128)(2,1)} %get-tuple-element.10), calls=%async_computation | async-start | bytes 2097152 | tf_op jit(solution)/shard_map/all_to_all | solution.py:398
  9.2 0.0 copy-start
  9.2 0.0 collective-permute-done
  9.2 0.0 copy-done.3
  9.2 1.2 %pad_maximum_fusion.near_ref = bf16[2,10,2,128,128]{4,3,2,1,0:T(8,128)(2,1)S(1)} fusion(bf16[2,5,2,128,128]{4,3,2,1,0:T(8,128)(2,1)} %collective-permute-done, bf16[2,5,2,128,128]{4,3,2,1,0:T(8,128)(2,1)S(1)} %bitcast.3), kind=kLoop, calls=%fused_computation | loop fusion | flops 655360 | bytes 2621440 | tf_op jit(solution)/shard_map/concatenate | solution.py:399
  10.4 0.0 copy-start.2
  10.4 0.0 copy-done
  10.4 0.6 %shard_map.65 = bf16[2,2,128,128]{3,2,1,0:T(8,128)(2,1)S(1)} custom-call(s32[2,18]{1,0:T(2,128)S(1)} %copy-done, bf16[2,10,2,128,128]{4,3,2,1,0:T(8,128)(2,1)S(1)} %pad_maximum_fusion.near_ref), custom_call_target="tpu_custom_call" | custom-call | bytes 300000 | tf_op jit(solution)/shard_map/pallas_call | solution.py:190
  11.1 2.1 %collective-permute-start.1 = (bf16[2,2,128,128]{3,2,1,0:T(8,128)(2,1)S(1)}, bf16[2,2,128,128]{3,2,1,0:T(8,128)(2,1)S(1)}, u32[]{:S(2)}, u32[]{:S(2)}) collective-permute-start(bf16[2,2,128,128]{3,2,1,0:T(8,128)(2,1)S(1)} %shard_map.65), channel_id=1, source_target_pairs={{0,2},{1,3},{2,0},{3,1},{4,6},{5,7},{6,4},{7,5},{8,10},{9,11},{10,... | collective-permute-start | bytes 393224 | tf_op jit(solution)/shard_map/ppermute | solution.py:170
  13.1 13.3 %collective-permute-done.1.far_ref = bf16[2,2,128,128]{3,2,1,0:T(8,128)(2,1)S(1)} collective-permute-done((bf16[2,2,128,128]{3,2,1,0:T(8,128)(2,1)S(1)}, bf16[2,2,128,128]{3,2,1,0:T(8,128)(2,1)S(1)}, u32[]{:S(2)}, u32[]{:S(2)}) %collective-permute-start.1) | collective-permute-done | bytes 131104 | tf_op jit(solution)/shard_map/ppermute | solution.py:170
  26.5 0.0 all-to-all-done.x_ref
  26.5 0.0 copy-done.2
  26.5 1.7 %shard_map.67 = bf16[2,2,128,128]{3,2,1,0:T(8,128)(2,1)S(1)} custom-call(s32[2,18]{1,0:T(2,128)S(1)} %copy-done, s32[2,18]{1,0:T(2,128)S(1)} %copy-done.2, bf16[8,2,2,128,128]{4,3,2,1,0:T(8,128)(2,1)S(1)} %all-to-all-done.x_ref, bf16[2,10,2,128,128]{4,3,2,1,0:T(8,128)(2,1)S(1)} %pad_maximum_fusion.near_ref, ...), custom_call_target="tpu_custom_call" | custom-call | flops 335544320 | bytes 524288 | tf_op jit(solution)/shard_map/pallas_call | solution.py:288
  28.2 2.7 %collective-permute-start.2 = (bf16[2,2,128,128]{3,2,1,0:T(8,128)(2,1)S(1)}, bf16[2,2,128,128]{3,2,1,0:T(8,128)(2,1)S(1)}, u32[]{:S(2)}, u32[]{:S(2)}) collective-permute-start(bf16[2,2,128,128]{3,2,1,0:T(8,128)(2,1)S(1)} %shard_map.67), channel_id=1, source_target_pairs={{0,16},{8,24},{16,0},{24,8},{1,17},{9,25},{17,1},{25,9},{2,18},{10... | collective-permute-start | bytes 393224 | tf_op jit(solution)/shard_map/ppermute | solution.py:405
  30.8 1.7 %shard_map.66.own_ref = f32[2,2,128,128]{3,2,1,0:T(8,128)S(1)} custom-call(s32[2,18]{1,0:T(2,128)S(1)} %copy-done, s32[2,18]{1,0:T(2,128)S(1)} %copy-done.2, bf16[8,2,2,128,128]{4,3,2,1,0:T(8,128)(2,1)S(1)} %all-to-all-done.x_ref, bf16[2,10,2,128,128]{4,3,2,1,0:T(8,128)(2,1)S(1)} %pad_maximum_fusion.near_ref, ...), custom_call_target="tpu_custom_call" | custom-call | flops 335544320 | bytes 524288 | tf_op jit(solution)/shard_map/pallas_call | solution.py:288
  32.5 0.0 copy-start.1
  32.5 4.5 %collective-permute-done.2.arrived_ref = bf16[2,2,128,128]{3,2,1,0:T(8,128)(2,1)S(1)} collective-permute-done((bf16[2,2,128,128]{3,2,1,0:T(8,128)(2,1)S(1)}, bf16[2,2,128,128]{3,2,1,0:T(8,128)(2,1)S(1)}, u32[]{:S(2)}, u32[]{:S(2)}) %collective-permute-start.2) | collective-permute-done | bytes 131104 | tf_op jit(solution)/shard_map/ppermute | solution.py:405
  37.0 1.8 %collective-permute-start.3 = (bf16[2,2,128,128]{3,2,1,0:T(8,128)(2,1)S(1)}, bf16[2,2,128,128]{3,2,1,0:T(8,128)(2,1)S(1)}, u32[]{:S(2)}, u32[]{:S(2)}) collective-permute-start(bf16[2,2,128,128]{3,2,1,0:T(8,128)(2,1)S(1)} %shard_map.68), channel_id=1, source_target_pairs={{0,4},{4,0},{1,5},{5,1},{2,6},{6,2},{3,7},{7,3},{8,12},{12,8},{9,1... | collective-permute-start | bytes 393224 | tf_op jit(solution)/shard_map/ppermute | solution.py:328
  38.9 3.2 %collective-permute-done.3 = bf16[2,2,128,128]{3,2,1,0:T(8,128)(2,1)S(1)} collective-permute-done((bf16[2,2,128,128]{3,2,1,0:T(8,128)(2,1)S(1)}, bf16[2,2,128,128]{3,2,1,0:T(8,128)(2,1)S(1)}, u32[]{:S(2)}, u32[]{:S(2)}) %collective-permute-start.3) | collective-permute-done | bytes 131104 | tf_op jit(solution)/shard_map/ppermute | solution.py:328
  42.1 1.0 %collective-permute-start.4 = (bf16[2,2,128,128]{3,2,1,0:T(8,128)(2,1)S(1)}, bf16[2,2,128,128]{3,2,1,0:T(8,128)(2,1)S(1)}, u32[]{:S(2)}, u32[]{:S(2)}) collective-permute-start(bf16[2,2,128,128]{3,2,1,0:T(8,128)(2,1)S(1)} %slice.3), channel_id=1, source_target_pairs={{0,2},{1,3},{2,0},{3,1},{4,6},{5,7},{6,4},{7,5},{8,10},{9,11},{10,... | collective-permute-start | bytes 393224 | tf_op jit(solution)/shard_map/ppermute | solution.py:170
  43.1 4.0 %collective-permute-done.4 = bf16[2,2,128,128]{3,2,1,0:T(8,128)(2,1)S(1)} collective-permute-done((bf16[2,2,128,128]{3,2,1,0:T(8,128)(2,1)S(1)}, bf16[2,2,128,128]{3,2,1,0:T(8,128)(2,1)S(1)}, u32[]{:S(2)}, u32[]{:S(2)}) %collective-permute-start.4) | collective-permute-done | bytes 131104 | tf_op jit(solution)/shard_map/ppermute | solution.py:170
  47.2 0.1 collective-permute-start.5
  47.2 1.7 %collective-permute-done.5.other_ref = bf16[6,2,128,128]{3,2,1,0:T(8,128)(2,1)S(1)} collective-permute-done((bf16[6,2,128,128]{3,2,1,0:T(8,128)(2,1)S(1)}, bf16[6,2,128,128]{3,2,1,0:T(8,128)(2,1)S(1)}, u32[]{:S(2)}, u32[]{:S(2)}) %collective-permute-start.5) | collective-permute-done | bytes 393248 | tf_op jit(solution)/shard_map/ppermute | solution.py:170
  49.0 0.0 copy-done.1
  49.0 1.4 %shard_map.69 = bf16[5,2,128,128]{3,2,1,0:T(8,128)(2,1)} custom-call(s32[2,18]{1,0:T(2,128)S(1)} %copy-done, s32[1,2,4]{2,1,0:T(2,128)S(1)} %copy-done.1, bf16[6,2,128,128]{3,2,1,0:T(8,128)(2,1)S(1)} %pad_maximum_fusion.1.same_ref, bf16[6,2,128,128]{3,2,1,0:T(8,128)(2,1)S(1)} %collective-permute-done.5.other_ref), custom_call_target="tpu_custom_call" | custom-call | bytes 1000000 | tf_op jit(solution)/shard_map/pallas_call | solution.py:373
  (4 shorter events, 0.1 us)
Async XLA Ops:
  0.0 9.2 %collective-permute-start = (bf16[2,5,2,128,128]{4,3,2,1,0:T(8,128)(2,1)}, bf16[2,5,2,128,128]{4,3,2,1,0:T(8,128)(2,1)}, u32[]{:S(2)}, u32[]{:S(2)}) collective-permute-start(bf16[2,5,2,128,128]{4,3,2,1,0:T(8,128)(2,1)} %bitcast.2), channel_id=1, source_target_pairs={{0,1},{1,0},{2,3},{3,2},{4,5},{5,4},{6,7},{7,6},{8,9},{9,8},{10,11... | collective-permute-start | bytes 1966088 | tf_op jit(solution)/shard_map/ppermute | solution.py:170
  4.2 5.0 %copy-start.3 = (bf16[1,2,5,2,128,128]{5,4,3,2,1,0:T(8,128)(2,1)S(1)}, bf16[1,2,5,2,128,128]{5,4,3,2,1,0:T(8,128)(2,1)}, u32[]{:S(2)}) copy-start(bf16[1,2,5,2,128,128]{5,4,3,2,1,0:T(8,128)(2,1)} %param.8) | copy-start | bytes 1966084
  4.2 22.3 %all-to-all-start = ((bf16[8,2,2,128,128]{4,3,2,1,0:T(8,128)(2,1)}), bf16[8,2,2,128,128]{4,3,2,1,0:T(8,128)(2,1)S(1)}, u32[]{:S(2)}, u32[]{:S(2)}) async-start(bf16[8,2,2,128,128]{4,3,2,1,0:T(8,128)(2,1)} %get-tuple-element.10), calls=%async_computation | async-start | bytes 2097152 | tf_op jit(solution)/shard_map/all_to_all | solution.py:398
  9.2 1.2 %copy-start = (s32[2,18]{1,0:T(2,128)S(1)}, s32[2,18]{1,0:T(2,128)}, u32[]{:S(2)}) copy-start(s32[2,18]{1,0:T(2,128)} %get-tuple-element.8.order_ref) | copy-start | bytes 436
  10.4 16.0 %copy-start.2 = (s32[2,18]{1,0:T(2,128)S(1)}, s32[2,18]{1,0:T(2,128)}, u32[]{:S(2)}) copy-start(s32[2,18]{1,0:T(2,128)} %get-tuple-element.9.flags_ref) | copy-start | bytes 436
  11.1 15.4 %collective-permute-start.1 = (bf16[2,2,128,128]{3,2,1,0:T(8,128)(2,1)S(1)}, bf16[2,2,128,128]{3,2,1,0:T(8,128)(2,1)S(1)}, u32[]{:S(2)}, u32[]{:S(2)}) collective-permute-start(bf16[2,2,128,128]{3,2,1,0:T(8,128)(2,1)S(1)} %shard_map.65), channel_id=1, source_target_pairs={{0,2},{1,3},{2,0},{3,1},{4,6},{5,7},{6,4},{7,5},{8,10},{9,11},{10,... | collective-permute-start | bytes 393224 | tf_op jit(solution)/shard_map/ppermute | solution.py:170
  28.2 8.8 %collective-permute-start.2 = (bf16[2,2,128,128]{3,2,1,0:T(8,128)(2,1)S(1)}, bf16[2,2,128,128]{3,2,1,0:T(8,128)(2,1)S(1)}, u32[]{:S(2)}, u32[]{:S(2)}) collective-permute-start(bf16[2,2,128,128]{3,2,1,0:T(8,128)(2,1)S(1)} %shard_map.67), channel_id=1, source_target_pairs={{0,16},{8,24},{16,0},{24,8},{1,17},{9,25},{17,1},{25,9},{2,18},{10... | collective-permute-start | bytes 393224 | tf_op jit(solution)/shard_map/ppermute | solution.py:405
  32.5 16.5 %copy-start.1 = (s32[1,2,4]{2,1,0:T(2,128)S(1)}, s32[1,2,4]{2,1,0:T(2,128)}, u32[]{:S(2)}) copy-start(s32[1,2,4]{2,1,0:T(2,128)} %counts_ref.3) | copy-start | bytes 100
  37.0 5.0 %collective-permute-start.3 = (bf16[2,2,128,128]{3,2,1,0:T(8,128)(2,1)S(1)}, bf16[2,2,128,128]{3,2,1,0:T(8,128)(2,1)S(1)}, u32[]{:S(2)}, u32[]{:S(2)}) collective-permute-start(bf16[2,2,128,128]{3,2,1,0:T(8,128)(2,1)S(1)} %shard_map.68), channel_id=1, source_target_pairs={{0,4},{4,0},{1,5},{5,1},{2,6},{6,2},{3,7},{7,3},{8,12},{12,8},{9,1... | collective-permute-start | bytes 393224 | tf_op jit(solution)/shard_map/ppermute | solution.py:328
  42.1 5.0 %collective-permute-start.4 = (bf16[2,2,128,128]{3,2,1,0:T(8,128)(2,1)S(1)}, bf16[2,2,128,128]{3,2,1,0:T(8,128)(2,1)S(1)}, u32[]{:S(2)}, u32[]{:S(2)}) collective-permute-start(bf16[2,2,128,128]{3,2,1,0:T(8,128)(2,1)S(1)} %slice.3), channel_id=1, source_target_pairs={{0,2},{1,3},{2,0},{3,1},{4,6},{5,7},{6,4},{7,5},{8,10},{9,11},{10,... | collective-permute-start | bytes 393224 | tf_op jit(solution)/shard_map/ppermute | solution.py:170
  47.2 1.8 %collective-permute-start.5 = (bf16[6,2,128,128]{3,2,1,0:T(8,128)(2,1)S(1)}, bf16[6,2,128,128]{3,2,1,0:T(8,128)(2,1)S(1)}, u32[]{:S(2)}, u32[]{:S(2)}) collective-permute-start(bf16[6,2,128,128]{3,2,1,0:T(8,128)(2,1)S(1)} %pad_maximum_fusion.1.same_ref), channel_id=1, source_target_pairs={{0,1},{1,0},{2,3},{3,2},{4,5},{5,4},{6,7},{7,6},{8,9},{9,8},{10,11... | collective-permute-start | bytes 1179656 | tf_op jit(solution)/shard_map/ppermute | solution.py:170

commit v3 on v2

--- a/solution.py
+++ b/solution.py
@@ -26,8 +26,8 @@
     tangent = jnp.tanh(tanh_scale * (hidden + cubic_coef * hidden * square))
     half = 0.5 * (1.0 + tangent)
     value = hidden * half
-    slope = half + 0.5 * hidden * (1.0 - tangent * tangent) * tanh_scale * (
-        1.0 + 3.0 * cubic_coef * square
+    slope = half + value * (1.0 - half) * (
+        2.0 * tanh_scale + 6.0 * tanh_scale * cubic_coef * square
     )
     return (value, slope)
 

time: 50.7 us -> 50.8 us (level)
  waiting for transfers between devices: 26.7 us -> 27.9 us
  starting transfers between devices: 13.1 us -> 12.2 us
    ppermute x1, waiting for transfers between devices: 3.19 us -> 3.78 us  [hand_round(): lax.ppermute(mine, 'dp', [(i, (i + by) % replicas) for i in range(replica...]
    ppermute x1, starting transfers between devices: 1.85 us -> 1.26 us  [hand_round(): lax.ppermute(mine, 'dp', [(i, (i + by) % replicas) for i in range(replica...]
where the time goes in v3:
time: 50.8 us; the launch traced here: 50.6 us
  waiting for transfers between devices  27.9 us (55%)
  starting transfers between devices  12.2 us (24%)
  Pallas kernels  9.13 us (18%)
  other arithmetic  1.28 us (3%)
    ppermute x4, waiting for transfers between devices, swapped(): return lax.ppermute(array, 'fsdp', [(i, i ^ apart) for i in range(size)])  19.4 us
    all_to_all x1, starting transfers between devices, body(): lax.all_to_all(packed, PLANE, split_axis=0, concat_axis=0, tiled=True)  4.98 us
    ppermute x1, waiting for transfers between devices, body(): arrived = lax.ppermute(grads(1, dtype=jnp.bfloat16), 'section', across)  4.72 us
    ppermute x1, waiting for transfers between devices, hand_round(): lax.ppermute(mine, 'dp', [(i, (i + by) % replicas) for i in range(replica...  3.78 us
    pallas_call x1, Pallas kernels, pack(): pl.pallas_call(functools.partial(pack_kernel, per_half), out_shape=[jax.S...  3.74 us
    pallas_call x2, Pallas kernels, unit_grads(): pl.pallas_call(functools.partial(grads_kernel, which, per_half, owners, l...  3.37 us
    ppermute x4, starting transfers between devices, swapped(): return lax.ppermute(array, 'fsdp', [(i, i ^ apart) for i in range(size)])  3.32 us
    ppermute x1, starting transfers between devices, body(): arrived = lax.ppermute(grads(1, dtype=jnp.bfloat16), 'section', across)  2.65 us
  transfers between devices with their start and end apart: 7, of which 5 were waited for; matrix products, arithmetic and copies ran while one was open for 2% of the time, Pallas kernels for 12%

profile of v3, /device:TPU:0, one launch (start us, length us, event | category | flops | bytes accessed | tf_op | source)
XLA Modules:
  0.0 50.6 jit_solution(16247712158932300506)
XLA Ops:
  0.0 0.5 collective-permute-start
  0.5 3.7 %shard_map.64 = (bf16[8,2,2,128,128]{4,3,2,1,0:T(8,128)(2,1)}, s32[2,18]{1,0:T(2,128)}, s32[2,18]{1,0:T(2,128)}) custom-call(s32[1,2,20]{2,1,0:T(2,128)} %rows_ref.1, s32[1,2,20]{2,1,0:T(2,128)} %cols_ref.1, s32[1,2,4]{2,1,0:T(2,128)} %counts_ref.3, bf16[1,1,128,6144]{3,2,1,0:T(8,128)(2,1)} %down_ref.1, bf16[1,1,128,6144]{3,2,1,0:T(8,128)(2,1)} %up_ref.1), custom_call_target="tpu_custom_call" | custom-call | bytes 5242880 | tf_op jit(solution)/shard_map/pallas_call | solution.py:148
  4.2 0.0 copy-start.3
  4.2 5.0 %all-to-all-start = ((bf16[8,2,2,128,128]{4,3,2,1,0:T(8,128)(2,1)}), bf16[8,2,2,128,128]{4,3,2,1,0:T(8,128)(2,1)S(1)}, u32[]{:S(2)}, u32[]{:S(2)}) async-start(bf16[8,2,2,128,128]{4,3,2,1,0:T(8,128)(2,1)} %get-tuple-element.10), calls=%async_computation | async-start | bytes 2097152 | tf_op jit(solution)/shard_map/all_to_all | solution.py:398
  9.2 0.0 copy-start
  9.2 0.0 collective-permute-done
  9.2 0.0 copy-done.3
  9.2 1.2 %pad_maximum_fusion.near_ref = bf16[2,10,2,128,128]{4,3,2,1,0:T(8,128)(2,1)S(1)} fusion(bf16[2,5,2,128,128]{4,3,2,1,0:T(8,128)(2,1)} %collective-permute-done, bf16[2,5,2,128,128]{4,3,2,1,0:T(8,128)(2,1)S(1)} %bitcast.3), kind=kLoop, calls=%fused_computation | loop fusion | flops 655360 | bytes 2621440 | tf_op jit(solution)/shard_map/concatenate | solution.py:399
  10.4 0.0 copy-start.2
  10.4 0.0 copy-done
  10.4 0.6 %shard_map.65 = bf16[2,2,128,128]{3,2,1,0:T(8,128)(2,1)S(1)} custom-call(s32[2,18]{1,0:T(2,128)S(1)} %copy-done, bf16[2,10,2,128,128]{4,3,2,1,0:T(8,128)(2,1)S(1)} %pad_maximum_fusion.near_ref), custom_call_target="tpu_custom_call" | custom-call | bytes 300000 | tf_op jit(solution)/shard_map/pallas_call | solution.py:190
  11.1 2.1 %collective-permute-start.1 = (bf16[2,2,128,128]{3,2,1,0:T(8,128)(2,1)S(1)}, bf16[2,2,128,128]{3,2,1,0:T(8,128)(2,1)S(1)}, u32[]{:S(2)}, u32[]{:S(2)}) collective-permute-start(bf16[2,2,128,128]{3,2,1,0:T(8,128)(2,1)S(1)} %shard_map.65), channel_id=1, source_target_pairs={{0,2},{1,3},{2,0},{3,1},{4,6},{5,7},{6,4},{7,5},{8,10},{9,11},{10,... | collective-permute-start | bytes 393224 | tf_op jit(solution)/shard_map/ppermute | solution.py:170
  13.1 13.3 %collective-permute-done.1.far_ref = bf16[2,2,128,128]{3,2,1,0:T(8,128)(2,1)S(1)} collective-permute-done((bf16[2,2,128,128]{3,2,1,0:T(8,128)(2,1)S(1)}, bf16[2,2,128,128]{3,2,1,0:T(8,128)(2,1)S(1)}, u32[]{:S(2)}, u32[]{:S(2)}) %collective-permute-start.1) | collective-permute-done | bytes 131104 | tf_op jit(solution)/shard_map/ppermute | solution.py:170
  26.5 0.0 all-to-all-done.x_ref
  26.5 0.0 copy-done.2
  26.5 1.7 %shard_map.67 = bf16[2,2,128,128]{3,2,1,0:T(8,128)(2,1)S(1)} custom-call(s32[2,18]{1,0:T(2,128)S(1)} %copy-done, s32[2,18]{1,0:T(2,128)S(1)} %copy-done.2, bf16[8,2,2,128,128]{4,3,2,1,0:T(8,128)(2,1)S(1)} %all-to-all-done.x_ref, bf16[2,10,2,128,128]{4,3,2,1,0:T(8,128)(2,1)S(1)} %pad_maximum_fusion.near_ref, ...), custom_call_target="tpu_custom_call" | custom-call | flops 335544320 | bytes 524288 | tf_op jit(solution)/shard_map/pallas_call | solution.py:288
  28.2 2.7 %collective-permute-start.2 = (bf16[2,2,128,128]{3,2,1,0:T(8,128)(2,1)S(1)}, bf16[2,2,128,128]{3,2,1,0:T(8,128)(2,1)S(1)}, u32[]{:S(2)}, u32[]{:S(2)}) collective-permute-start(bf16[2,2,128,128]{3,2,1,0:T(8,128)(2,1)S(1)} %shard_map.67), channel_id=1, source_target_pairs={{0,16},{8,24},{16,0},{24,8},{1,17},{9,25},{17,1},{25,9},{2,18},{10... | collective-permute-start | bytes 393224 | tf_op jit(solution)/shard_map/ppermute | solution.py:405
  30.8 1.7 %shard_map.66.own_ref = f32[2,2,128,128]{3,2,1,0:T(8,128)S(1)} custom-call(s32[2,18]{1,0:T(2,128)S(1)} %copy-done, s32[2,18]{1,0:T(2,128)S(1)} %copy-done.2, bf16[8,2,2,128,128]{4,3,2,1,0:T(8,128)(2,1)S(1)} %all-to-all-done.x_ref, bf16[2,10,2,128,128]{4,3,2,1,0:T(8,128)(2,1)S(1)} %pad_maximum_fusion.near_ref, ...), custom_call_target="tpu_custom_call" | custom-call | flops 335544320 | bytes 524288 | tf_op jit(solution)/shard_map/pallas_call | solution.py:288
  32.5 0.0 copy-start.1
  32.5 4.7 %collective-permute-done.2.arrived_ref = bf16[2,2,128,128]{3,2,1,0:T(8,128)(2,1)S(1)} collective-permute-done((bf16[2,2,128,128]{3,2,1,0:T(8,128)(2,1)S(1)}, bf16[2,2,128,128]{3,2,1,0:T(8,128)(2,1)S(1)}, u32[]{:S(2)}, u32[]{:S(2)}) %collective-permute-start.2) | collective-permute-done | bytes 131104 | tf_op jit(solution)/shard_map/ppermute | solution.py:405
  37.3 1.3 %collective-permute-start.3 = (bf16[2,2,128,128]{3,2,1,0:T(8,128)(2,1)S(1)}, bf16[2,2,128,128]{3,2,1,0:T(8,128)(2,1)S(1)}, u32[]{:S(2)}, u32[]{:S(2)}) collective-permute-start(bf16[2,2,128,128]{3,2,1,0:T(8,128)(2,1)S(1)} %shard_map.68), channel_id=1, source_target_pairs={{0,4},{4,0},{1,5},{5,1},{2,6},{6,2},{3,7},{7,3},{8,12},{12,8},{9,1... | collective-permute-start | bytes 393224 | tf_op jit(solution)/shard_map/ppermute | solution.py:328
  38.5 3.8 %collective-permute-done.3 = bf16[2,2,128,128]{3,2,1,0:T(8,128)(2,1)S(1)} collective-permute-done((bf16[2,2,128,128]{3,2,1,0:T(8,128)(2,1)S(1)}, bf16[2,2,128,128]{3,2,1,0:T(8,128)(2,1)S(1)}, u32[]{:S(2)}, u32[]{:S(2)}) %collective-permute-start.3) | collective-permute-done | bytes 131104 | tf_op jit(solution)/shard_map/ppermute | solution.py:328
  42.4 0.7 %collective-permute-start.4 = (bf16[2,2,128,128]{3,2,1,0:T(8,128)(2,1)S(1)}, bf16[2,2,128,128]{3,2,1,0:T(8,128)(2,1)S(1)}, u32[]{:S(2)}, u32[]{:S(2)}) collective-permute-start(bf16[2,2,128,128]{3,2,1,0:T(8,128)(2,1)S(1)} %slice.3), channel_id=1, source_target_pairs={{0,2},{1,3},{2,0},{3,1},{4,6},{5,7},{6,4},{7,5},{8,10},{9,11},{10,... | collective-permute-start | bytes 393224 | tf_op jit(solution)/shard_map/ppermute | solution.py:170
  43.1 4.3 %collective-permute-done.4 = bf16[2,2,128,128]{3,2,1,0:T(8,128)(2,1)S(1)} collective-permute-done((bf16[2,2,128,128]{3,2,1,0:T(8,128)(2,1)S(1)}, bf16[2,2,128,128]{3,2,1,0:T(8,128)(2,1)S(1)}, u32[]{:S(2)}, u32[]{:S(2)}) %collective-permute-start.4) | collective-permute-done | bytes 131104 | tf_op jit(solution)/shard_map/ppermute | solution.py:170
  47.4 0.1 collective-permute-start.5
  47.5 1.7 %collective-permute-done.5.other_ref = bf16[6,2,128,128]{3,2,1,0:T(8,128)(2,1)S(1)} collective-permute-done((bf16[6,2,128,128]{3,2,1,0:T(8,128)(2,1)S(1)}, bf16[6,2,128,128]{3,2,1,0:T(8,128)(2,1)S(1)}, u32[]{:S(2)}, u32[]{:S(2)}) %collective-permute-start.5) | collective-permute-done | bytes 393248 | tf_op jit(solution)/shard_map/ppermute | solution.py:170
  49.2 0.0 copy-done.1
  49.2 1.4 %shard_map.69 = bf16[5,2,128,128]{3,2,1,0:T(8,128)(2,1)} custom-call(s32[2,18]{1,0:T(2,128)S(1)} %copy-done, s32[1,2,4]{2,1,0:T(2,128)S(1)} %copy-done.1, bf16[6,2,128,128]{3,2,1,0:T(8,128)(2,1)S(1)} %pad_maximum_fusion.1.same_ref, bf16[6,2,128,128]{3,2,1,0:T(8,128)(2,1)S(1)} %collective-permute-done.5.other_ref), custom_call_target="tpu_custom_call" | custom-call | bytes 1000000 | tf_op jit(solution)/shard_map/pallas_call | solution.py:373
  (4 shorter events, 0.1 us)
Async XLA Ops:
  0.0 9.2 %collective-permute-start = (bf16[2,5,2,128,128]{4,3,2,1,0:T(8,128)(2,1)}, bf16[2,5,2,128,128]{4,3,2,1,0:T(8,128)(2,1)}, u32[]{:S(2)}, u32[]{:S(2)}) collective-permute-start(bf16[2,5,2,128,128]{4,3,2,1,0:T(8,128)(2,1)} %bitcast.2), channel_id=1, source_target_pairs={{0,1},{1,0},{2,3},{3,2},{4,5},{5,4},{6,7},{7,6},{8,9},{9,8},{10,11... | collective-permute-start | bytes 1966088 | tf_op jit(solution)/shard_map/ppermute | solution.py:170
  4.2 5.0 %copy-start.3 = (bf16[1,2,5,2,128,128]{5,4,3,2,1,0:T(8,128)(2,1)S(1)}, bf16[1,2,5,2,128,128]{5,4,3,2,1,0:T(8,128)(2,1)}, u32[]{:S(2)}) copy-start(bf16[1,2,5,2,128,128]{5,4,3,2,1,0:T(8,128)(2,1)} %param.8) | copy-start | bytes 1966084
  4.2 22.3 %all-to-all-start = ((bf16[8,2,2,128,128]{4,3,2,1,0:T(8,128)(2,1)}), bf16[8,2,2,128,128]{4,3,2,1,0:T(8,128)(2,1)S(1)}, u32[]{:S(2)}, u32[]{:S(2)}) async-start(bf16[8,2,2,128,128]{4,3,2,1,0:T(8,128)(2,1)} %get-tuple-element.10), calls=%async_computation | async-start | bytes 2097152 | tf_op jit(solution)/shard_map/all_to_all | solution.py:398
  9.2 1.2 %copy-start = (s32[2,18]{1,0:T(2,128)S(1)}, s32[2,18]{1,0:T(2,128)}, u32[]{:S(2)}) copy-start(s32[2,18]{1,0:T(2,128)} %get-tuple-element.8.order_ref) | copy-start | bytes 436
  10.4 16.0 %copy-start.2 = (s32[2,18]{1,0:T(2,128)S(1)}, s32[2,18]{1,0:T(2,128)}, u32[]{:S(2)}) copy-start(s32[2,18]{1,0:T(2,128)} %get-tuple-element.9.flags_ref) | copy-start | bytes 436
  11.1 15.4 %collective-permute-start.1 = (bf16[2,2,128,128]{3,2,1,0:T(8,128)(2,1)S(1)}, bf16[2,2,128,128]{3,2,1,0:T(8,128)(2,1)S(1)}, u32[]{:S(2)}, u32[]{:S(2)}) collective-permute-start(bf16[2,2,128,128]{3,2,1,0:T(8,128)(2,1)S(1)} %shard_map.65), channel_id=1, source_target_pairs={{0,2},{1,3},{2,0},{3,1},{4,6},{5,7},{6,4},{7,5},{8,10},{9,11},{10,... | collective-permute-start | bytes 393224 | tf_op jit(solution)/shard_map/ppermute | solution.py:170
  28.2 9.1 %collective-permute-start.2 = (bf16[2,2,128,128]{3,2,1,0:T(8,128)(2,1)S(1)}, bf16[2,2,128,128]{3,2,1,0:T(8,128)(2,1)S(1)}, u32[]{:S(2)}, u32[]{:S(2)}) collective-permute-start(bf16[2,2,128,128]{3,2,1,0:T(8,128)(2,1)S(1)} %shard_map.67), channel_id=1, source_target_pairs={{0,16},{8,24},{16,0},{24,8},{1,17},{9,25},{17,1},{25,9},{2,18},{10... | collective-permute-start | bytes 393224 | tf_op jit(solution)/shard_map/ppermute | solution.py:405
  32.5 16.7 %copy-start.1 = (s32[1,2,4]{2,1,0:T(2,128)S(1)}, s32[1,2,4]{2,1,0:T(2,128)}, u32[]{:S(2)}) copy-start(s32[1,2,4]{2,1,0:T(2,128)} %counts_ref.3) | copy-start | bytes 100
  37.3 5.0 %collective-permute-start.3 = (bf16[2,2,128,128]{3,2,1,0:T(8,128)(2,1)S(1)}, bf16[2,2,128,128]{3,2,1,0:T(8,128)(2,1)S(1)}, u32[]{:S(2)}, u32[]{:S(2)}) collective-permute-start(bf16[2,2,128,128]{3,2,1,0:T(8,128)(2,1)S(1)} %shard_map.68), channel_id=1, source_target_pairs={{0,4},{4,0},{1,5},{5,1},{2,6},{6,2},{3,7},{7,3},{8,12},{12,8},{9,1... | collective-permute-start | bytes 393224 | tf_op jit(solution)/shard_map/ppermute | solution.py:328
  42.4 5.0 %collective-permute-start.4 = (bf16[2,2,128,128]{3,2,1,0:T(8,128)(2,1)S(1)}, bf16[2,2,128,128]{3,2,1,0:T(8,128)(2,1)S(1)}, u32[]{:S(2)}, u32[]{:S(2)}) collective-permute-start(bf16[2,2,128,128]{3,2,1,0:T(8,128)(2,1)S(1)} %slice.3), channel_id=1, source_target_pairs={{0,2},{1,3},{2,0},{3,1},{4,6},{5,7},{6,4},{7,5},{8,10},{9,11},{10,... | collective-permute-start | bytes 393224 | tf_op jit(solution)/shard_map/ppermute | solution.py:170
  47.4 1.8 %collective-permute-start.5 = (bf16[6,2,128,128]{3,2,1,0:T(8,128)(2,1)S(1)}, bf16[6,2,128,128]{3,2,1,0:T(8,128)(2,1)S(1)}, u32[]{:S(2)}, u32[]{:S(2)}) collective-permute-start(bf16[6,2,128,128]{3,2,1,0:T(8,128)(2,1)S(1)} %pad_maximum_fusion.1.same_ref), channel_id=1, source_target_pairs={{0,1},{1,0},{2,3},{3,2},{4,5},{5,4},{6,7},{7,6},{8,9},{9,8},{10,11... | collective-permute-start | bytes 1179656 | tf_op jit(solution)/shard_map/ppermute | solution.py:170
